TPU v7x, 256 devices: a whole 4x4x8 slice. The times are simulated.
256 devices in a mesh: seg: 32 (over x, z), term: 8 (over y, core).
Axes of the slice: x: 4, y: 4, z: 8, core: 2. Of those that a mesh axis runs over, the one named last changes fastest.
Arguments:
- left_blocks: bfloat16 [32, 32, 512, 512], P('seg', 'term'), may hold values from -0.25 to 0.25
- right_blocks: bfloat16 [32, 32, 512, 512], P('seg', 'term'), may hold values from -0.046875 to 0.046875
- start_state: float32 [32, 512, 512], P('seg'), may hold values from -6 to 6
- left_transfer: float32 [32, 512, 512], P('seg'), as said below
- right_transfer: float32 [32, 512, 512], P('seg'), as said below
- ranks: int32 [32, 2], P('seg'), may hold values from 128 to 512
Outputs:
- final_state: float32 [32, 512, 512], P('seg')
Inputs may be any that keep to these rules, and one draw needn't show every extreme that they name: `left_transfer`: entries of size about 0.3 / sqrt(512). `right_transfer`: entries of size about 0.3 / sqrt(512).
All inputs are finite; a program needn't handle non-finite values.
Results may differ from a plain program's by a relative error of at most 0.008.
Values may be sent and summed in bfloat16 or wider, within the bound.
A program may use at most 128 MiB of HBM per device.

v0:
```python
import jax
import jax.numpy as jnp
from jax import lax
from jax.sharding import PartitionSpec as P

ITERS = 2


def prefix(part, axis, combine, identity, reverse):
    count = lax.axis_size(axis)
    place = lax.axis_index(axis)
    ahead = count - 1 - place if reverse else place
    gathered = lax.all_gather(part, axis)
    state = jnp.zeros_like(part) + jnp.asarray(identity, part.dtype)

    def one(lap, state):
        source = count - 1 - lap if reverse else lap
        return combine(state, lax.dynamic_index_in_dim(gathered, source, 0, False))

    return lax.fori_loop(0, ahead, one, state)


def passed_along(shard, axis, by):
    length = lax.axis_size(axis)
    pairs = [(i, i + by) for i in range(length) if 0 <= i + by < length]
    return lax.ppermute(shard, axis, pairs)


def normed(block, target):
    return block * (target / jnp.sqrt(jnp.sum(block * block) + 1e-06))


def combine_env(earlier, later):
    root = float(earlier.shape[0]) ** 0.5
    return normed(jnp.dot(earlier, later, precision=lax.Precision.HIGHEST), root)


def term_partial(left_ops, right_ops, moved):
    inner = jnp.einsum("tij,jk->tik", left_ops, moved, preferred_element_type=jnp.float32).astype(
        jnp.bfloat16
    )
    return jnp.einsum("tik,tlk->il", inner, right_ops, preferred_element_type=jnp.float32)


def half_sweep(left_ops, right_ops, basis, start, live_mask):
    block_size = start.shape[0]
    basis_b = basis.astype(jnp.bfloat16)
    basis_wide = basis_b.astype(jnp.float32)
    state = normed(start * live_mask, float(block_size))
    for step_index in range(ITERS):
        state_b = state.astype(jnp.bfloat16)
        moved = jnp.dot(basis_b, state_b, preferred_element_type=jnp.float32).astype(jnp.bfloat16)
        partial_sum = term_partial(left_ops, right_ops, moved)
        term_total = lax.psum(partial_sum, "term")
        applied = lax.dot_general(
            basis_wide, term_total, (((0,), (0,)), ((), ())), precision=lax.Precision.HIGHEST
        )
        state = normed((2.0 * state - applied) * live_mask, float(block_size))
    return state


def per_device(left_blocks, right_blocks, start_state, left_transfer, right_transfer, ranks):
    block_size = start_state.shape[-1]
    unit_matrix = jnp.eye(block_size, dtype=jnp.float32)
    root = float(block_size) ** 0.5
    left_unit = normed(unit_matrix + left_transfer[0], root)
    right_unit = normed(unit_matrix + right_transfer[0], root)
    left_env = prefix(left_unit, "seg", combine_env, unit_matrix, False)
    right_env = prefix(right_unit, "seg", combine_env, unit_matrix, True)
    positions = jnp.arange(block_size)
    rows_live = (positions < ranks[0, 0]).astype(jnp.float32)
    cols_live = (positions < ranks[0, 1]).astype(jnp.float32)
    live_mask = rows_live[:, None] * cols_live[None, :]
    first_state = half_sweep(left_blocks[0], right_blocks[0], left_env, start_state[0], live_mask)
    neighbour = passed_along(first_state.astype(jnp.bfloat16), "seg", 1)
    seeded = first_state + 0.5 * neighbour.astype(jnp.float32)
    flipped = half_sweep(right_blocks[0], left_blocks[0], right_env.T, seeded.T, live_mask.T)
    return flipped.T[None]


def solution(mesh):
    in_specs = (
        P("seg", "term", None, None),
        P("seg", "term", None, None),
        P("seg", None, None),
        P("seg", None, None),
        P("seg", None, None),
        P("seg", None),
    )
    out_specs = P("seg", None, None)
    return jax.shard_map(
        per_device, mesh=mesh, in_specs=in_specs, out_specs=out_specs, check_vma=False
    )
```

profile of v0, /device:TPU:2, one launch (start us, length us, event | category | flops | bytes accessed | tf_op | source)
XLA Modules:
  0.0 1196.1 jit_solution(1782328151539934472)
XLA Ops:
  20.8 227.6 %all-gather.3.cloned.1.call-done = f32[32,512,512]{2,1,0:T(8,128)} async-done(((f32[1,512,512]{2,1,0:T(8,128)}), f32[32,512,512]{2,1,0:T(8,128)}) %all-gather.3.cloned.1.call-update) | async-done | bytes 33554448 | tf_op jit(solution)/shard_map/all_gather | solution.py:13
  248.4 47.2 %while.22 = (s32[]{:T(128)}, f32[512,512]{0,1:T(8,128)}, s32[]{:T(128)}, f32[32,512,512]{2,1,0:T(8,128)}, s32[]{:T(128)}, /*index=5*/s32[]{:T(128)}, s32[]{:T(128)}, f32[]{:T(128)}, f32[]{:T(128)}) while((s32[]{:T(128)}, f32[512,512]{0,1:T(8,128)}, s32[]{:T(128)}, f32[32,512,512]{2,1,0:T(8,128)}, s32[]{:T(128)}, /*index=5*/s32[]{:T(128)}, ...), condition=%wide.region_4.5_spmd, body=%wide.region_2.4_spmd.sunk | while | flops 1611399168 | bytes 5243051 | solution.py:20
  248.4 4.1 multiply_reduce_fusion.9
  254.3 4.2 multiply_reduce_fusion.9
  260.2 4.1 multiply_reduce_fusion.9
  266.1 4.2 multiply_reduce_fusion.9
  272.0 4.1 multiply_reduce_fusion.9
  277.9 4.2 multiply_reduce_fusion.9
  283.8 4.1 multiply_reduce_fusion.9
  289.7 4.2 multiply_reduce_fusion.9
  296.9 5.2 fusion.28
  313.6 193.5 %all-reduce.5.cloned.1.call-done = f32[512,512]{1,0:T(8,128)} async-done(((f32[512,512]{1,0:T(8,128)}), f32[512,512]{1,0:T(8,128)}) %all-reduce.5.cloned.1.call-update) | async-done | bytes 1048592 | tf_op jit(solution)/shard_map/psum | solution.py:54
  507.2 4.4 multiply_reduce_fusion.5
  512.3 5.1 fusion.31
  530.9 59.2 %all-reduce.7.cloned.1.call-done = f32[512,512]{1,0:T(8,128)} async-done(((f32[512,512]{1,0:T(8,128)}), f32[512,512]{1,0:T(8,128)}) %all-reduce.7.cloned.1.call-update) | async-done | bytes 1048592 | tf_op jit(solution)/shard_map/psum | solution.py:54
  590.1 4.4 multiply_reduce_fusion.4
  597.3 3.5 collective-permute-start
  600.8 228.4 %all-gather.5.cloned.1.call-done = f32[32,512,512]{2,1,0:T(8,128)} async-done(((f32[1,512,512]{2,1,0:T(8,128)}), f32[32,512,512]{2,1,0:T(8,128)}) %all-gather.5.cloned.1.call-update) | async-done | bytes 33554448 | tf_op jit(solution)/shard_map/all_gather | solution.py:13
  829.2 134.0 %while.23 = (s32[]{:T(128)}, f32[512,512]{0,1:T(8,128)}, s32[]{:T(128)}, f32[32,512,512]{2,1,0:T(8,128)}, s32[]{:T(128)}, /*index=5*/s32[]{:T(128)}, s32[]{:T(128)}, s32[]{:T(128)}, f32[]{:T(128)}, f32[]{:T(128)}) while((s32[]{:T(128)}, f32[512,512]{0,1:T(8,128)}, s32[]{:T(128)}, f32[32,512,512]{2,1,0:T(8,128)}, s32[]{:T(128)}, ...), condition=%wide.region_13.14_spmd, body=%wide.region_11.13_spmd.sunk | while | flops 1611399168 | bytes 5243071 | solution.py:20
  829.2 4.1 multiply_reduce_fusion.10
  835.1 4.1 multiply_reduce_fusion.10
  840.9 4.1 multiply_reduce_fusion.10
  846.7 4.1 multiply_reduce_fusion.10
  852.5 4.1 multiply_reduce_fusion.10
  858.4 4.1 multiply_reduce_fusion.10
  864.2 4.1 multiply_reduce_fusion.10
  870.0 4.1 multiply_reduce_fusion.10
  875.8 4.1 multiply_reduce_fusion.10
  881.7 4.1 multiply_reduce_fusion.10
  887.5 4.1 multiply_reduce_fusion.10
  893.3 4.1 multiply_reduce_fusion.10
  899.1 4.1 multiply_reduce_fusion.10
  905.0 4.1 multiply_reduce_fusion.10
  910.8 4.1 multiply_reduce_fusion.10
  916.6 4.1 multiply_reduce_fusion.10
  922.4 4.1 multiply_reduce_fusion.10
  928.3 4.1 multiply_reduce_fusion.10
  934.1 4.1 multiply_reduce_fusion.10
  939.9 4.1 multiply_reduce_fusion.10
  945.7 4.1 multiply_reduce_fusion.10
  951.6 4.1 multiply_reduce_fusion.10
  957.4 4.1 multiply_reduce_fusion.10
  968.2 4.2 fusion.34
  978.0 109.2 %all-reduce.9.cloned.1.call-done = f32[512,512]{1,0:T(8,128)} async-done(((f32[512,512]{1,0:T(8,128)}), f32[512,512]{1,0:T(8,128)}) %all-reduce.9.cloned.1.call-update) | async-done | bytes 1048592 | tf_op jit(solution)/shard_map/psum | solution.py:54
  1087.2 3.4 fusion.102
  1097.1 4.4 fusion.37
  1108.6 65.8 %all-reduce.11.cloned.1.call-done = f32[512,512]{1,0:T(8,128)} async-done(((f32[512,512]{1,0:T(8,128)}), f32[512,512]{1,0:T(8,128)}) %all-reduce.11.cloned.1.call-update) | async-done | bytes 1048592 | tf_op jit(solution)/shard_map/psum | solution.py:54
  1174.4 3.5 fusion.103
  (100 shorter events, 107.0 us)
Async XLA Ops:
  6.5 298.8 %copy-start = (bf16[1,4,512,512]{3,2,1,0:T(8,128)(2,1)S(1)}, bf16[1,4,512,512]{3,2,1,0:T(8,128)(2,1)}, u32[]{:S(2)}) copy-start(bf16[1,4,512,512]{3,2,1,0:T(8,128)(2,1)} %param.11) | copy-start | bytes 6291460
  6.5 5.6 copy-start.7
  6.5 241.9 %all-gather.3.cloned.1.call-start = ((), (), s32[]{:S(2)}) async-start(), calls=%async_computation | async-start | bytes 34603008 | tf_op jit(solution)/shard_map/all_gather | solution.py:13
  13.3 1.6 copy-start.8
  13.3 493.8 %all-reduce.5.cloned.1.call-start = ((), (), s32[]{:S(2)}) async-start(), calls=%async_computation.1 | async-start | bytes 2097152 | tf_op jit(solution)/shard_map/psum | solution.py:54
  14.9 5.8 copy-start.3
  18.8 1.0 copy-start.1
  296.9 5.2 copy-start.6
  305.4 2.6 copy-start.4
  307.8 282.3 %all-reduce.7.cloned.1.call-start = ((), (), s32[]{:S(2)}) async-start(), calls=%async_computation.2 | async-start | bytes 2097152 | tf_op jit(solution)/shard_map/psum | solution.py:54
  523.0 306.2 %all-gather.5.cloned.1.call-start = ((), (), s32[]{:S(2)}) async-start(), calls=%async_computation.3 | async-start | bytes 34603008 | tf_op jit(solution)/shard_map/all_gather | solution.py:13
  530.9 556.4 %all-reduce.9.cloned.1.call-start = ((), (), s32[]{:S(2)}) async-start(), calls=%async_computation.4 | async-start | bytes 2097152 | tf_op jit(solution)/shard_map/psum | solution.py:54
  597.3 368.0 %collective-permute-start = (bf16[512,512]{1,0:T(8,128)(2,1)}, bf16[512,512]{1,0:T(8,128)(2,1)}, u32[]{:S(2)}, u32[]{:S(2)}) collective-permute-start(bf16[512,512]{1,0:T(8,128)(2,1)} %multiply_convert_fusion.2), channel_id=1, source_target_pairs={{0,8},{8,16},{16,24},{24,32},{32,40},{40,48},{48,56},{56,64},{64,7... | collective-permute-start | bytes 1572872 | tf_op jit(solution)/shard_map/ppermute | solution.py:26
  963.2 2.2 copy-start.2
  972.3 3.4 copy-start.9
  978.0 196.4 %all-reduce.11.cloned.1.call-start = ((), (), s32[]{:S(2)}) async-start(), calls=%async_computation.5 | async-start | bytes 2097152 | tf_op jit(solution)/shard_map/psum | solution.py:54
  1101.6 3.4 copy-start.10
  1177.8 5.9 copy-start.5
Sparse Core Ops, SparseCore 0:
  13.4 234.9 all-gather.2
  307.9 199.2 all-reduce.4
  523.1 66.9 all-reduce.6
  592.5 236.6 all-gather.4
  978.1 109.0 all-reduce.8
  1107.4 66.9 all-reduce.10
where the time goes:
time: 1200 us
  waiting for transfers between devices  884 us (74%)
  matrix products  172 us (14%)
  other arithmetic  61.5 us (5%)
  local copies, waits for them, and re-layouts  35.8 us (3%)
  loops' own time  19.7 us (2%)
  between operations  19.3 us (2%)
    all_gather x2, waiting for transfers between devices, prefix(): gathered = lax.all_gather(part, axis)  456 us
    psum x4, waiting for transfers between devices, half_sweep(): term_total = lax.psum(partial_sum, 'term')  428 us
    dot_general x31, matrix products, combine_env(): jnp.dot(earlier, later, precision=lax.Precision.HIGHEST)  128 us
    mul x33, other arithmetic, normed(): return block * (target / jnp.sqrt(jnp.sum(block * block) + 1e-06))  36.7 us
  transfers between devices with their start and end apart: 7, of which 6 were waited for; matrix products, arithmetic and copies ran while one was open for 12% of the time, Pallas kernels for 0%

commit v1 on v0

--- a/solution.py
+++ b/solution.py
@@ -2,8 +2,14 @@
 import jax.numpy as jnp
 from jax import lax
 from jax.sharding import PartitionSpec as P
+from jax.lax import all_gather
 
 ITERS = 2
+
+
+def reach_ports(along_axis, raw):
+    s_next = all_gather(raw, axis_name=along_axis).sum(axis=0)
+    return s_next
 
 
 def prefix(part, axis, combine, identity, reverse):
@@ -51,7 +57,7 @@
         state_b = state.astype(jnp.bfloat16)
         moved = jnp.dot(basis_b, state_b, preferred_element_type=jnp.float32).astype(jnp.bfloat16)
         partial_sum = term_partial(left_ops, right_ops, moved)
-        term_total = lax.psum(partial_sum, "term")
+        term_total = reach_ports("term", partial_sum)
         applied = lax.dot_general(
             basis_wide, term_total, (((0,), (0,)), ((), ())), precision=lax.Precision.HIGHEST
         )

time: 1200 us -> 1150 us (0.958)
  waiting for transfers between devices: 884 us -> 826 us
  other arithmetic: 61.5 us -> 82.2 us
  local copies, waits for them, and re-layouts: 35.8 us -> 22.1 us
    psum x4 -> x0, waiting for transfers between devices: 428 us -> none  [half_sweep(): term_total = lax.psum(partial_sum, 'term')]
    all_gather x0 -> x4, waiting for transfers between devices: none -> 369 us  [reach_ports(): s_next = all_gather(raw, axis_name=along_axis).sum(axis=0)]
    reduce_sum x0 -> x4, other arithmetic: none -> 22 us  [reach_ports(): s_next = all_gather(raw, axis_name=along_axis).sum(axis=0)]
    unnamed x30 -> x28, local copies, waits for them, and re-layouts: 21.9 us -> 9.65 us
  transfers between devices with their start and end apart: 7 -> 7, of which waited for: 6 -> 6; matrix products, arithmetic and copies ran while one was open for 12% -> 13% of each run, Pallas kernels for 0% -> 0%
where the time goes in v1:
time: 1150 us
  waiting for transfers between devices  826 us (72%)
  matrix products  174 us (15%)
  other arithmetic  82.2 us (7%)
  local copies, waits for them, and re-layouts  22.1 us (2%)
  loops' own time  20.8 us (2%)
  between operations  18.7 us (2%)
    all_gather x2, waiting for transfers between devices, prefix(): gathered = lax.all_gather(part, axis)  457 us
    all_gather x4, waiting for transfers between devices, reach_ports(): s_next = all_gather(raw, axis_name=along_axis).sum(axis=0)  369 us
    dot_general x31, matrix products, combine_env(): jnp.dot(earlier, later, precision=lax.Precision.HIGHEST)  129 us
    mul x33, other arithmetic, normed(): return block * (target / jnp.sqrt(jnp.sum(block * block) + 1e-06))  36.9 us
  transfers between devices with their start and end apart: 7, of which 6 were waited for; matrix products, arithmetic and copies ran while one was open for 13% of the time, Pallas kernels for 0%

profile of v1, /device:TPU:2, one launch (start us, length us, event | category | flops | bytes accessed | tf_op | source)
XLA Modules:
  0.0 1148.2 jit_solution(4828620765279658668)
XLA Ops:
  20.3 227.8 %all-gather.11.cloned.1.call-done = f32[32,512,512]{2,1,0:T(8,128)} async-done(((f32[1,512,512]{2,1,0:T(8,128)}), f32[32,512,512]{2,1,0:T(8,128)}) %all-gather.11.cloned.1.call-update) | async-done | bytes 33554448 | tf_op jit(solution)/shard_map/all_gather | solution.py:19
  248.2 47.2 %while.22 = (s32[]{:T(128)}, f32[512,512]{0,1:T(8,128)}, s32[]{:T(128)}, f32[32,512,512]{2,1,0:T(8,128)}, s32[]{:T(128)}, /*index=5*/s32[]{:T(128)}, s32[]{:T(128)}, f32[]{:T(128)}, f32[]{:T(128)}) while((s32[]{:T(128)}, f32[512,512]{0,1:T(8,128)}, s32[]{:T(128)}, f32[32,512,512]{2,1,0:T(8,128)}, s32[]{:T(128)}, /*index=5*/s32[]{:T(128)}, ...), condition=%wide.region_4.5_spmd, body=%wide.region_2.4_spmd.sunk | while | flops 1611399168 | bytes 5243051 | solution.py:26
  248.2 4.2 multiply_reduce_fusion.9
  254.1 4.2 multiply_reduce_fusion.9
  260.0 4.2 multiply_reduce_fusion.9
  265.9 4.2 multiply_reduce_fusion.9
  271.8 4.2 multiply_reduce_fusion.9
  277.7 4.2 multiply_reduce_fusion.9
  283.6 4.2 multiply_reduce_fusion.9
  289.5 4.2 multiply_reduce_fusion.9
  300.1 5.2 fusion.48
  311.0 178.7 %all-gather.15.cloned.1.call-done = f32[4096,512]{1,0:T(8,128)} async-done(((f32[512,512]{1,0:T(8,128)}), f32[4096,512]{1,0:T(8,128)}) %all-gather.15.cloned.1.call-update) | async-done | bytes 8388624 | tf_op jit(solution)/shard_map/all_gather | solution.py:11
  489.6 5.6 reduce_sum.131
  495.3 4.5 multiply_reduce_fusion.5
  502.1 4.9 fusion.55
  515.0 44.7 %all-gather.17.cloned.1.call-done = f32[4096,512]{1,0:T(8,128)} async-done(((f32[512,512]{1,0:T(8,128)}), f32[4096,512]{1,0:T(8,128)}) %all-gather.17.cloned.1.call-update) | async-done | bytes 8388624 | tf_op jit(solution)/shard_map/all_gather | solution.py:11
  559.7 5.5 reduce_sum.133
  565.1 4.6 multiply_reduce_fusion.4
  576.0 229.1 %all-gather.13.cloned.1.call-done = f32[32,512,512]{2,1,0:T(8,128)} async-done(((f32[1,512,512]{2,1,0:T(8,128)}), f32[32,512,512]{2,1,0:T(8,128)}) %all-gather.13.cloned.1.call-update) | async-done | bytes 33554448 | tf_op jit(solution)/shard_map/all_gather | solution.py:19
  805.1 135.6 %while.23 = (s32[]{:T(128)}, f32[512,512]{0,1:T(8,128)}, s32[]{:T(128)}, f32[32,512,512]{2,1,0:T(8,128)}, s32[]{:T(128)}, /*index=5*/s32[]{:T(128)}, s32[]{:T(128)}, s32[]{:T(128)}, f32[]{:T(128)}, f32[]{:T(128)}) while((s32[]{:T(128)}, f32[512,512]{0,1:T(8,128)}, s32[]{:T(128)}, f32[32,512,512]{2,1,0:T(8,128)}, s32[]{:T(128)}, ...), condition=%wide.region_13.14_spmd, body=%wide.region_11.13_spmd.sunk | while | flops 1611399168 | bytes 5243071 | solution.py:26
  805.1 4.1 multiply_reduce_fusion.10
  811.0 4.1 multiply_reduce_fusion.10
  816.9 4.1 multiply_reduce_fusion.10
  822.8 4.1 multiply_reduce_fusion.10
  828.7 4.1 multiply_reduce_fusion.10
  834.6 4.1 multiply_reduce_fusion.10
  840.5 4.1 multiply_reduce_fusion.10
  846.4 4.1 multiply_reduce_fusion.10
  852.3 4.1 multiply_reduce_fusion.10
  858.2 4.1 multiply_reduce_fusion.10
  864.1 4.1 multiply_reduce_fusion.10
  870.0 4.1 multiply_reduce_fusion.10
  875.9 4.1 multiply_reduce_fusion.10
  881.8 4.1 multiply_reduce_fusion.10
  887.7 4.1 multiply_reduce_fusion.10
  893.6 4.1 multiply_reduce_fusion.10
  899.5 4.1 multiply_reduce_fusion.10
  905.4 4.1 multiply_reduce_fusion.10
  911.2 4.1 multiply_reduce_fusion.10
  917.1 4.1 multiply_reduce_fusion.10
  923.0 4.1 multiply_reduce_fusion.10
  934.8 4.1 multiply_reduce_fusion.10
  948.1 5.1 fusion.62
  953.5 94.3 %all-gather.19.cloned.1.call-done = f32[4096,512]{1,0:T(8,128)} async-done(((f32[512,512]{1,0:T(8,128)}), f32[4096,512]{1,0:T(8,128)}) %all-gather.19.cloned.1.call-update) | async-done | bytes 8388624 | tf_op jit(solution)/shard_map/all_gather | solution.py:11
  1047.8 5.5 reduce_sum.137
  1065.6 5.1 fusion.69
  1072.0 51.3 %all-gather.21.cloned.1.call-done = f32[4096,512]{1,0:T(8,128)} async-done(((f32[512,512]{1,0:T(8,128)}), f32[4096,512]{1,0:T(8,128)}) %all-gather.21.cloned.1.call-update) | async-done | bytes 8388624 | tf_op jit(solution)/shard_map/all_gather | solution.py:11
  1123.3 5.5 reduce_sum.139
  (102 shorter events, 106.9 us)
Async XLA Ops:
  6.5 293.6 %copy-start = (bf16[1,4,512,512]{3,2,1,0:T(8,128)(2,1)S(1)}, bf16[1,4,512,512]{3,2,1,0:T(8,128)(2,1)}, u32[]{:S(2)}) copy-start(bf16[1,4,512,512]{3,2,1,0:T(8,128)(2,1)} %param.11) | copy-start | bytes 6291460
  6.5 5.4 copy-start.9
  6.5 241.6 %all-gather.11.cloned.1.call-start = ((), (), s32[]{:S(2)}) async-start(), calls=%async_computation | async-start | bytes 34603008 | tf_op jit(solution)/shard_map/all_gather | solution.py:19
  13.1 1.6 copy-start.11
  13.1 476.6 %all-gather.15.cloned.1.call-start = ((), (), s32[]{:S(2)}) async-start(), calls=%async_computation.2 | async-start | bytes 9437184 | tf_op jit(solution)/shard_map/all_gather | solution.py:11
  14.7 5.6 copy-start.2
  18.4 1.0 copy-start.1
  296.7 0.8 copy-start.4
  300.1 5.3 copy-start.3
  305.4 254.3 %all-gather.17.cloned.1.call-start = ((), (), s32[]{:S(2)}) async-start(), calls=%async_computation.3 | async-start | bytes 9437184 | tf_op jit(solution)/shard_map/all_gather | solution.py:11
  307.0 2.7 copy-start.10
  489.6 5.6 copy-start.5
  507.0 298.1 %all-gather.13.cloned.1.call-start = ((), (), s32[]{:S(2)}) async-start(), calls=%async_computation.1 | async-start | bytes 34603008 | tf_op jit(solution)/shard_map/all_gather | solution.py:19
  514.8 533.0 %all-gather.19.cloned.1.call-start = ((), (), s32[]{:S(2)}) async-start(), calls=%async_computation.4 | async-start | bytes 9437184 | tf_op jit(solution)/shard_map/all_gather | solution.py:11
  572.5 370.4 %collective-permute-start = (bf16[512,512]{1,0:T(8,128)(2,1)}, bf16[512,512]{1,0:T(8,128)(2,1)}, u32[]{:S(2)}, u32[]{:S(2)}) collective-permute-start(bf16[512,512]{1,0:T(8,128)(2,1)} %multiply_convert_fusion.2), channel_id=1, source_target_pairs={{0,8},{8,16},{16,24},{24,32},{32,40},{40,48},{48,56},{56,64},{64,7... | collective-permute-start | bytes 1572872 | tf_op jit(solution)/shard_map/ppermute | solution.py:32
  940.7 2.2 copy-start.7
  953.2 170.1 %all-gather.21.cloned.1.call-start = ((), (), s32[]{:S(2)}) async-start(), calls=%async_computation.5 | async-start | bytes 9437184 | tf_op jit(solution)/shard_map/all_gather | solution.py:11
  1123.3 5.5 copy-start.6
  1132.1 2.7 copy-start.8
Sparse Core Ops, SparseCore 0:
  13.2 234.9 all-gather.10
  305.5 184.0 all-gather.14
  507.2 52.4 all-gather.16
  562.1 242.9 all-gather.12
  953.3 94.4 all-gather.18
  1070.8 52.4 all-gather.20
